TPU v7x, 32 devices: a whole 2x2x4 slice. The times are simulated.
32 devices in a mesh: gx: 4 (over y, x), gy: 8 (over z, core).
Axes of the slice: x: 2, y: 2, z: 4, core: 2. Of those that a mesh axis runs over, the one named last changes fastest.
Arguments:
- source: float32 [2, 256, 64, 512], P(None, ('gx', 'gy')), may hold values from -6 to 6
- weights: float32 [5, 2, 256, 64, 128], P(None, None, ('gx', 'gy')), may hold values from -0.375 to 0.375
- interp: float32 [2, 256, 64, 128], P(None, ('gx', 'gy')), may hold values from -0.5 to 0.5
Outputs:
- far_field: float32 [2, 512, 256, 128], P(None, ('gx', 'gy'))
All inputs are finite; a program needn't handle non-finite values.
Results may differ from a plain program's by a relative error of at most 0.0001.
Values sent between devices are 32-bit elements; how exact they have to be, the bound alone decides.
A program may use at most 64 MiB of HBM per device.

v0:
```python
import functools

import jax
import jax.numpy as jnp
from jax import lax
from jax.experimental import pallas as pl
from jax.experimental.pallas import tpu as pltpu
from jax.sharding import PartitionSpec as P

MESH = pl.DeviceIdType.MESH
BF = jnp.bfloat16
F32 = jnp.float32


def split(x):
    hi = x.astype(BF)
    return hi, (x - hi.astype(F32)).astype(BF)


def mul3(x, both, width):
    hi, lo = split(x)
    wide = jnp.dot(hi, both, preferred_element_type=F32)
    return wide[:, :width] + (
        wide[:, width:] + jnp.dot(lo, both[:, :width], preferred_element_type=F32)
    )


def kernel(ngx, ngy, halves, source, weights, interp, out, wp, ip, held, got, stage,
           send_sem, recv_sem, put_sem, take_sem, own_sem):
    n = ngx * ngy
    levels = weights.shape[0]
    boxes, rank, frames = source.shape[1:]
    q = interp.shape[3]
    per = frames // n // halves
    rows = frames // halves
    chunks = halves * boxes
    bits_gy = ngy.bit_length() - 1
    gx, gy = lax.axis_index("gx"), lax.axis_index("gy")
    me = gx * ngy + gy

    barrier = pltpu.get_barrier_semaphore()

    def greet(i, _):
        there = lax.rem(me + i, n)
        pl.semaphore_signal(barrier, inc=1, device_id=(lax.div(there, ngy), lax.rem(there, ngy)),
                            device_id_type=MESH)
        return 0

    lax.fori_loop(1, n, greet, 0)

    def bit_of(level):
        if level < bits_gy:
            return lax.rem(lax.div(gy, 2**level), 2)
        return lax.rem(lax.div(gx, 2 ** (level - bits_gy)), 2)

    def exchange(level, c):
        bit = bit_of(level)
        if level < bits_gy:
            there = (gx, gy + 2**level * (1 - 2 * bit))
        else:
            there = (gx + 2 ** (level - bits_gy) * (1 - 2 * bit), gy)
        return pltpu.make_async_remote_copy(
            src_ref=held.at[level, c], dst_ref=got.at[level, c],
            send_sem=send_sem.at[level, c], recv_sem=recv_sem.at[level, c],
            device_id=there, device_id_type=MESH)

    def prepare(level, k):
        real, imag = weights[level, 0, k], weights[level, 1, k]
        p = jnp.concatenate([real, imag], axis=0).T
        m = jnp.concatenate([-imag, real], axis=0).T
        low = jnp.concatenate([p[:rank], m[:rank]], axis=0)
        high = jnp.concatenate([p[rank:], m[rank:]], axis=0)
        first = bit_of(level) == 0
        own = jnp.where(first, low, high)
        other = jnp.where(first, high, low)
        hi, lo = split(jnp.concatenate([own, other], axis=0))
        wp[level, k] = jnp.concatenate([hi, lo], axis=1)

    def prepare_interp(k):
        real, imag = interp[0, k], interp[1, k]
        top = jnp.concatenate([real, imag], axis=1)
        low = jnp.concatenate([-imag, real], axis=1)
        hi, lo = split(jnp.concatenate([top, low], axis=0))
        ip[k] = jnp.concatenate([hi, lo], axis=1)

    def put(h, i):
        there = lax.rem(me + i, n)
        return pltpu.make_async_remote_copy(
            src_ref=stage.at[h, :, pl.ds(there * per, per)],
            dst_ref=out.at[:, pl.ds(h * per, per), pl.ds(me * boxes, boxes)],
            send_sem=put_sem.at[h, i], recv_sem=take_sem.at[h, me],
            device_id=(lax.div(there, ngy), lax.rem(there, ngy)), device_id_type=MESH)

    def take(h, i):
        there = lax.rem(me + i, n)
        return pltpu.make_async_remote_copy(
            src_ref=stage.at[h, :, pl.ds(there * per, per)],
            dst_ref=out.at[:, pl.ds(h * per, per), pl.ds(there * boxes, boxes)],
            send_sem=put_sem.at[h, i], recv_sem=take_sem.at[h, there],
            device_id=(lax.div(there, ngy), lax.rem(there, ngy)), device_id_type=MESH)

    def keep(h):
        return pltpu.make_async_copy(
            stage.at[h, :, pl.ds(me * per, per)],
            out.at[:, pl.ds(h * per, per), pl.ds(me * boxes, boxes)], own_sem.at[h])

    def turn(k, _):
        state = jnp.concatenate([source[0, k], source[1, k]], axis=0).T
        if halves == 1:
            held[0, k] = state
        else:
            state = state.reshape(n, halves, per, 2 * rank)
            for h in range(halves):
                held[0, h * boxes + k] = state[:, h].reshape(rows, 2 * rank)
        return 0

    lax.fori_loop(0, boxes, turn, 0)
    pl.semaphore_wait(barrier, n - 1)

    def first(c, _):
        exchange(0, c).start()
        return 0

    lax.fori_loop(0, chunks, first, 0)

    def work(level, c):
        h, k = lax.div(c, boxes), lax.rem(c, boxes)

        @pl.when(h == 0)
        def _():
            prepare(level, k)
            if level == levels - 1:
                prepare_interp(k)

        exchange(level, c).wait_recv()
        both = jnp.concatenate([held[level, c], got[level, c]], axis=1)
        state = mul3(both, wp[level, k], 2 * rank)
        if level < levels - 1:
            held[level + 1, c] = state
            exchange(level + 1, c).start()
            return
        samples = mul3(state, ip[k], 2 * q)
        for part in range(2):
            flat = stage.at[h, part].reshape(rows * boxes, q)
            flat[pl.ds(k, rows, stride=boxes), :] = samples[:, part * q:(part + 1) * q]

        @pl.when(k == boxes - 1)
        def _():
            def send(i, _):
                put(h, i).start()
                return 0

            lax.fori_loop(1, n, send, 0)
            keep(h).start()

    ahead, apart = 4, 2
    lag = [0] + [ahead + apart * (level - 1) for level in range(1, levels)]

    def tick(t, _):
        for level in range(levels):
            c = t - lag[level]

            @pl.when((t >= lag[level]) & (t < lag[level] + chunks))
            def _():
                work(level, c)

        return 0

    lax.fori_loop(0, chunks + lag[-1], tick, 0)

    def finish(c, _):
        for level in range(levels):
            exchange(level, c).wait_send()
        return 0

    lax.fori_loop(0, chunks, finish, 0)
    for h in range(halves):
        def end(i, _):
            put(h, i).wait_send()
            take(h, i).wait_recv()
            return 0

        lax.fori_loop(1, n, end, 0)
        keep(h).wait()


def solution(mesh):
    ngx, ngy = mesh.shape["gx"], mesh.shape["gy"]
    n = ngx * ngy

    def on_device(source, weights, interp):
        _, boxes, rank, frames = source.shape
        levels = weights.shape[0]
        q = interp.shape[3]
        each = frames // n
        halves = 2 if each % 16 == 0 else 1
        rows = frames // halves
        chunks = halves * boxes
        vmem = pl.BlockSpec(memory_space=pltpu.VMEM)
        return pl.pallas_call(
            functools.partial(kernel, ngx, ngy, halves),
            out_shape=jax.ShapeDtypeStruct((2, each, n * boxes, q), F32),
            in_specs=[vmem] * 3,
            out_specs=pl.BlockSpec(memory_space=pl.ANY),
            scratch_shapes=[
                pltpu.VMEM((levels, boxes, 4 * rank, 4 * rank), BF),
                pltpu.VMEM((boxes, 2 * rank, 4 * q), BF),
                pltpu.VMEM((levels, chunks, rows, 2 * rank), F32),
                pltpu.VMEM((levels, chunks, rows, 2 * rank), F32),
                pltpu.VMEM((halves, 2, rows, boxes, q), F32),
                pltpu.SemaphoreType.DMA((levels, chunks)),
                pltpu.SemaphoreType.DMA((levels, chunks)),
                pltpu.SemaphoreType.DMA((halves, n)),
                pltpu.SemaphoreType.DMA((halves, n)),
                pltpu.SemaphoreType.DMA((halves,)),
            ],
            compiler_params=pltpu.CompilerParams(
                collective_id=0, has_side_effects=True, vmem_limit_bytes=56 * 2**20),
        )(source, weights, interp)

    return jax.shard_map(
        on_device,
        mesh=mesh,
        in_specs=(
            P(None, ("gx", "gy"), None, None),
            P(None, None, ("gx", "gy"), None, None),
            P(None, ("gx", "gy"), None, None),
        ),
        out_specs=P(None, ("gx", "gy"), None, None),
        check_vma=False,
    )
```

profile of v0, /device:TPU:1, one launch (start us, length us, event | category | flops | bytes accessed | tf_op | source)
XLA Modules:
  0.0 220.6 jit_solution(3212786619111178931)
XLA Ops:
  0.0 215.9 %shard_map.37 = f32[2,16,256,128]{3,2,1,0:T(8,128)} custom-call(f32[2,8,64,512]{3,2,1,0:T(8,128)} %source.1, f32[5,2,8,64,128]{4,3,2,1,0:T(8,128)} %weights.1, f32[2,8,64,128]{3,2,1,0:T(8,128)} %interp.1), custom_call_target="tpu_custom_call" | custom-call | tf_op jit(solution)/shard_map/pallas_call | solution.py:200
  215.9 4.7 %copy.5 = f32[2,16,256,128]{3,2,1,0:T(8,128)} copy(f32[2,16,256,128]{3,2,1,0:T(8,128)} %shard_map.37) | data formatting | bytes 8388608
where the time goes:
time: 224 us; the launch traced here: 221 us
  Pallas kernels  216 us (96%)
  local copies, waits for them, and re-layouts  4.65 us (2%)
    pallas_call x1, Pallas kernels, on_device(): pl.pallas_call(functools.partial(kernel, ngx, ngy, halves), out_shape=jax...  216 us
    unnamed x1, local copies, waits for them, and re-layouts  4.65 us

commit v1 on v0

v1 whole, which is shorter than its diff:
```python
import functools

import jax
import jax.numpy as jnp
from jax import lax
from jax.experimental import pallas as pl
from jax.experimental.pallas import tpu as pltpu
from jax.sharding import PartitionSpec as P

MESH = pl.DeviceIdType.MESH
BF = jnp.bfloat16
F32 = jnp.float32
CORES = 2
SLOTS = 3


def split(x):
    hi = x.astype(BF)
    return hi, (x - hi.astype(F32)).astype(BF)


def mul3(x, both, width):
    hi, lo = split(x)
    wide = jnp.dot(hi, both, preferred_element_type=F32)
    return wide[:, :width] + (
        wide[:, width:] + jnp.dot(lo, both[:, :width], preferred_element_type=F32)
    )


def kernel(ngx, ngy, parts, source, weights, interp, out, wp, ip, held, got, zgot, igot,
           stage, turned, send_sem, recv_sem, zsend_sem, zrecv_sem, isend_sem, irecv_sem,
           put_sem, take_sem, own_sem):
    levels = weights.shape[0]
    boxes, rank, frames = source.shape[1:]
    q = interp.shape[3]
    nz = ngy // CORES
    plane = ngx * CORES
    each = frames // (ngx * ngy)
    per = each // parts
    rows = frames // parts
    zrows = rows // nz
    chunks = parts * boxes
    bits_gy = ngy.bit_length() - 1
    gx, gy = lax.axis_index("gx"), lax.axis_index("gy")
    z, core = lax.div(gy, CORES), lax.rem(gy, CORES)
    last = levels % SLOTS

    def at_z(where):
        return (gx, where * CORES + core)

    def in_plane(i):
        u = lax.rem(gx * CORES + core + i, plane)
        return lax.div(u, CORES), lax.rem(u, CORES)

    barrier = pltpu.get_barrier_semaphore()

    def greet_z(i, _):
        pl.semaphore_signal(barrier, inc=1, device_id=at_z(lax.rem(z + i, nz)),
                            device_id_type=MESH)
        return 0

    def greet_plane(i, _):
        x, c = in_plane(i)
        pl.semaphore_signal(barrier, inc=1, device_id=(x, z * CORES + c), device_id_type=MESH)
        return 0

    lax.fori_loop(1, nz, greet_z, 0)
    lax.fori_loop(1, plane, greet_plane, 0)

    def bit_of(level):
        if level < bits_gy:
            return lax.rem(lax.div(gy, 2**level), 2)
        return lax.rem(lax.div(gx, 2 ** (level - bits_gy)), 2)

    def exchange(level, c):
        bit = bit_of(level)
        if level < bits_gy:
            there = (gx, gy + 2**level * (1 - 2 * bit))
        else:
            there = (gx + 2 ** (level - bits_gy) * (1 - 2 * bit), gy)
        return pltpu.make_async_remote_copy(
            src_ref=held.at[level % SLOTS, c], dst_ref=got.at[level, c],
            send_sem=send_sem.at[level, c], recv_sem=recv_sem.at[level, c],
            device_id=there, device_id_type=MESH)

    def prepare(level, k):
        real, imag = weights[level, 0, k], weights[level, 1, k]
        p = jnp.concatenate([real, imag], axis=0).T
        m = jnp.concatenate([-imag, real], axis=0).T
        low = jnp.concatenate([p[:rank], m[:rank]], axis=0)
        high = jnp.concatenate([p[rank:], m[rank:]], axis=0)
        first = bit_of(level) == 0
        own = jnp.where(first, low, high)
        other = jnp.where(first, high, low)
        hi, lo = split(jnp.concatenate([own, other], axis=0))
        wp[level, k] = jnp.concatenate([hi, lo], axis=1)

    def prepare_interp(where, k):
        real, imag = igot[where, 0, k], igot[where, 1, k]
        top = jnp.concatenate([real, imag], axis=1)
        low = jnp.concatenate([-imag, real], axis=1)
        hi, lo = split(jnp.concatenate([top, low], axis=0))
        ip[where, k] = jnp.concatenate([hi, lo], axis=1)

    def pass_on(way, j):
        block = z - j if way == 0 else z + j
        there = z + 1 if way == 0 else z - 1
        return pltpu.make_async_remote_copy(
            src_ref=igot.at[block], dst_ref=igot.at[block],
            send_sem=isend_sem.at[way, j], recv_sem=irecv_sem.at[way, j + 1],
            device_id=at_z(there), device_id_type=MESH)

    def taken(way, j):
        block = z - j if way == 0 else z + j
        there = z - 1 if way == 0 else z + 1
        return pltpu.make_async_remote_copy(
            src_ref=igot.at[block], dst_ref=igot.at[block],
            send_sem=isend_sem.at[way, j - 1], recv_sem=irecv_sem.at[way, j],
            device_id=at_z(there), device_id_type=MESH)

    def sends(way, j):
        return ((z >= j) & (z + 1 < nz)) if way == 0 else ((z + j < nz) & (z >= 1))

    def takes(way, j):
        return (z >= j) if way == 0 else (z + j < nz)

    def gather_step(j):
        for way in range(2):
            if j > 0:
                @pl.when(takes(way, j))
                def _():
                    taken(way, j).wait_recv()
            if j < nz - 1:
                @pl.when(sends(way, j))
                def _():
                    pass_on(way, j).start()

    def over_z(c, j):
        there = lax.rem(z + j, nz)
        return pltpu.make_async_remote_copy(
            src_ref=held.at[last, c, pl.ds(pl.multiple_of(there * zrows, zrows), zrows)],
            dst_ref=zgot.at[c, z],
            send_sem=zsend_sem.at[c, j], recv_sem=zrecv_sem.at[c, z],
            device_id=at_z(there), device_id_type=MESH)

    def from_z(c, j):
        there = lax.rem(z + j, nz)
        return pltpu.make_async_remote_copy(
            src_ref=held.at[last, c, pl.ds(pl.multiple_of(there * zrows, zrows), zrows)],
            dst_ref=zgot.at[c, there],
            send_sem=zsend_sem.at[c, j], recv_sem=zrecv_sem.at[c, there],
            device_id=at_z(there), device_id_type=MESH)

    def put(h, i):
        x, c = in_plane(i)
        return pltpu.make_async_remote_copy(
            src_ref=stage.at[h, :, :, c, x],
            dst_ref=out.at[:, pl.ds(h * per, per), gx, :, core],
            send_sem=put_sem.at[h, i], recv_sem=take_sem.at[h, gx * CORES + core],
            device_id=(x, z * CORES + c), device_id_type=MESH)

    def take(h, i):
        x, c = in_plane(i)
        return pltpu.make_async_remote_copy(
            src_ref=stage.at[h, :, :, c, x],
            dst_ref=out.at[:, pl.ds(h * per, per), x, :, c],
            send_sem=put_sem.at[h, i], recv_sem=take_sem.at[h, x * CORES + c],
            device_id=(x, z * CORES + c), device_id_type=MESH)

    def keep(h):
        return pltpu.make_async_copy(
            stage.at[h, :, :, core, gx],
            out.at[:, pl.ds(h * per, per), gx, :, core], own_sem.at[h])

    def turn(k):
        turned[...] = jnp.concatenate([source[0, k], source[1, k]], axis=0).T
        for h in range(parts):
            for zz in range(nz):
                for i in range(per):
                    for c in range(CORES):
                        start = (zz * CORES + c) * each + h * per + i
                        to = zz * zrows + (i * CORES + c) * ngx
                        held[0, h * boxes + k, to:to + ngx, :] = turned[
                            pl.ds(start, ngx, stride=ngy * each), :]

    turn(0)
    igot[z] = interp[...]
    pl.semaphore_wait(barrier, nz - 1 + plane - 1)

    def begin(k, _):
        @pl.when(k > 0)
        def _():
            turn(k)

        for h in range(parts):
            exchange(0, h * boxes + k).start()
        return 0

    lax.fori_loop(0, boxes, begin, 0)

    def work(level, c):
        h, k = lax.div(c, boxes), lax.rem(c, boxes)

        @pl.when(h == 0)
        def _():
            prepare(level, k)

        exchange(level, c).wait_recv()
        both = jnp.concatenate([held[level % SLOTS, c], got[level, c]], axis=1)
        state = mul3(both, wp[level, k], 2 * rank)
        if level >= SLOTS - 1:
            exchange(level + 1 - SLOTS, c).wait_send()
        held[(level + 1) % SLOTS, c] = state
        if level < levels - 1:
            exchange(level + 1, c).start()
        else:
            for j in range(1, nz):
                over_z(c, j).start()
            zgot[c, z] = held[last, c, pl.ds(pl.multiple_of(z * zrows, zrows), zrows), :]

    def project(c):
        h, k = lax.div(c, boxes), lax.rem(c, boxes)

        @pl.when(h == 0)
        def _():
            for where in range(nz):
                prepare_interp(where, k)

        for j in range(1, nz):
            from_z(c, j).wait_recv()
        for where in range(nz):
            samples = mul3(zgot[c, where], ip[where, k], 2 * q)
            for part in range(2):
                flat = stage.at[h, part].reshape(rows * boxes, q)
                flat[pl.ds(where * boxes + k, zrows, stride=nz * boxes), :] = samples[
                    :, part * q:(part + 1) * q]

        @pl.when(k == boxes - 1)
        def _():
            def send(i, _):
                put(h, i).start()
                return 0

            lax.fori_loop(1, plane, send, 0)
            keep(h).start()

    ahead, apart = boxes, 3
    lag = [0] + [ahead + apart * (level - 1) for level in range(1, levels + 1)]

    def tick(t, _):
        for j in range(nz):
            @pl.when(t == j * lag[-1] // max(nz - 1, 1))
            def _():
                gather_step(j)

        for level in range(levels + 1):
            c = t - lag[level]

            @pl.when((t >= lag[level]) & (t < lag[level] + chunks))
            def _():
                if level < levels:
                    work(level, c)
                else:
                    project(c)

        return 0

    lax.fori_loop(0, chunks + lag[-1], tick, 0)

    def finish(c, _):
        for level in range(max(levels + 1 - SLOTS, 0), levels):
            exchange(level, c).wait_send()
        for j in range(1, nz):
            over_z(c, j).wait_send()
        return 0

    lax.fori_loop(0, chunks, finish, 0)
    for way in range(2):
        for j in range(nz - 1):
            @pl.when(sends(way, j))
            def _():
                pass_on(way, j).wait_send()

    def end(h, _):
        def one(i, _):
            put(h, i).wait_send()
            take(h, i).wait_recv()
            return 0

        lax.fori_loop(1, plane, one, 0)
        keep(h).wait()
        return 0

    lax.fori_loop(0, parts, end, 0)


def solution(mesh):
    ngx, ngy = mesh.shape["gx"], mesh.shape["gy"]
    n = ngx * ngy
    nz = ngy // CORES

    def on_device(source, weights, interp):
        _, boxes, rank, frames = source.shape
        levels = weights.shape[0]
        q = interp.shape[3]
        each = frames // n
        parts = 4 if each % 4 == 0 else 1
        rows = frames // parts
        chunks = parts * boxes
        vmem = pl.BlockSpec(memory_space=pltpu.VMEM)
        dma = pltpu.SemaphoreType.DMA
        result = pl.pallas_call(
            functools.partial(kernel, ngx, ngy, parts),
            out_shape=jax.ShapeDtypeStruct((2, each, ngx, nz, CORES, boxes, q), F32),
            in_specs=[vmem] * 3,
            out_specs=pl.BlockSpec(memory_space=pl.ANY),
            scratch_shapes=[
                pltpu.VMEM((levels, boxes, 4 * rank, 4 * rank), BF),
                pltpu.VMEM((nz, boxes, 2 * rank, 4 * q), BF),
                pltpu.VMEM((SLOTS, chunks, rows, 2 * rank), F32),
                pltpu.VMEM((levels, chunks, rows, 2 * rank), F32),
                pltpu.VMEM((chunks, nz, rows // nz, 2 * rank), F32),
                pltpu.VMEM((nz,) + interp.shape, F32),
                pltpu.VMEM((parts, 2, each // parts, CORES, ngx, nz, boxes, q), F32),
                pltpu.VMEM((frames, 2 * rank), F32),
                dma((levels, chunks)),
                dma((levels, chunks)),
                dma((chunks, nz)),
                dma((chunks, nz)),
                dma((2, nz)),
                dma((2, nz)),
                dma((parts, CORES * ngx)),
                dma((parts, CORES * ngx)),
                dma((parts,)),
            ],
            compiler_params=pltpu.CompilerParams(
                collective_id=0, has_side_effects=True, vmem_limit_bytes=60 * 2**20),
        )(source, weights, interp)
        return result.reshape(2, each, n * boxes, q)

    return jax.shard_map(
        on_device,
        mesh=mesh,
        in_specs=(
            P(None, ("gx", "gy"), None, None),
            P(None, None, ("gx", "gy"), None, None),
            P(None, ("gx", "gy"), None, None),
        ),
        out_specs=P(None, ("gx", "gy"), None, None),
        check_vma=False,
    )
```

time: 224 us -> 219 us (0.978)
  Pallas kernels: 216 us -> 213 us
    pallas_call x1, Pallas kernels: 216 us -> 213 us  [on_device(): pl.pallas_call(functools.partial(kernel, ngx, ngy, parts), out_shape=jax....]
where the time goes in v1:
time: 219 us; the launch traced here: 218 us
  Pallas kernels  213 us (97%)
  local copies, waits for them, and re-layouts  4.65 us (2%)
    pallas_call x1, Pallas kernels, on_device(): pl.pallas_call(functools.partial(kernel, ngx, ngy, parts), out_shape=jax....  213 us
    unnamed x1, local copies, waits for them, and re-layouts  4.65 us

profile of v1, /device:TPU:1, one launch (start us, length us, event | category | flops | bytes accessed | tf_op | source)
XLA Modules:
  0.0 217.6 jit_solution(4427622947605379891)
XLA Ops:
  0.0 212.9 %shard_map.37 = f32[2,16,4,4,2,8,128]{6,5,4,3,2,1,0:T(8,128)} custom-call(f32[2,8,64,512]{3,2,1,0:T(8,128)} %source.1, f32[5,2,8,64,128]{4,3,2,1,0:T(8,128)} %weights.1, f32[2,8,64,128]{3,2,1,0:T(8,128)} %interp.1), custom_call_target="tpu_custom_call" | custom-call | tf_op jit(solution)/shard_map/pallas_call | solution.py:312
  212.9 4.7 %copy.5 = f32[2,16,256,128]{3,2,1,0:T(8,128)} copy(f32[2,16,256,128]{3,2,1,0:T(8,128)} %bitcast.1) | data formatting | bytes 8388608

commit v2 on v1

--- a/solution.py
+++ b/solution.py
@@ -12,6 +12,7 @@
 F32 = jnp.float32
 CORES = 2
 SLOTS = 3
+GROUP = 2
 
 
 def split(x):
@@ -198,42 +199,56 @@
 
     lax.fori_loop(0, boxes, begin, 0)
 
-    def work(level, c):
-        h, k = lax.div(c, boxes), lax.rem(c, boxes)
-
-        @pl.when(h == 0)
+    def box(c):
+        return lax.div(c, boxes), lax.rem(c, boxes)
+
+    def work(level, step):
+        group = [step * GROUP + g for g in range(GROUP)]
+
+        @pl.when(step * GROUP < boxes)
         def _():
-            prepare(level, k)
-
-        exchange(level, c).wait_recv()
-        both = jnp.concatenate([held[level % SLOTS, c], got[level, c]], axis=1)
-        state = mul3(both, wp[level, k], 2 * rank)
-        if level >= SLOTS - 1:
-            exchange(level + 1 - SLOTS, c).wait_send()
-        held[(level + 1) % SLOTS, c] = state
-        if level < levels - 1:
-            exchange(level + 1, c).start()
-        else:
+            for c in group:
+                prepare(level, box(c)[1])
+
+        for c in group:
+            exchange(level, c).wait_recv()
+            if level >= SLOTS - 1:
+                exchange(level + 1 - SLOTS, c).wait_send()
+        both = [jnp.concatenate([held[level % SLOTS, c], got[level, c]], axis=1) for c in group]
+        blocks = [wp[level, box(c)[1]] for c in group]
+        states = [mul3(x, w, 2 * rank) for x, w in zip(both, blocks)]
+        for c, state in zip(group, states):
+            held[(level + 1) % SLOTS, c] = state
+        for c in group:
+            if level < levels - 1:
+                exchange(level + 1, c).start()
+            else:
+                for j in range(1, nz):
+                    over_z(c, j).start()
+                zgot[c, z] = held[last, c, pl.ds(pl.multiple_of(z * zrows, zrows), zrows), :]
+
+    def project(step):
+        group = [step * GROUP + g for g in range(GROUP)]
+
+        @pl.when(step * GROUP < boxes)
+        def _():
+            for c in group:
+                for where in range(nz):
+                    prepare_interp(where, box(c)[1])
+
+        for c in group:
             for j in range(1, nz):
-                over_z(c, j).start()
-            zgot[c, z] = held[last, c, pl.ds(pl.multiple_of(z * zrows, zrows), zrows), :]
-
-    def project(c):
-        h, k = lax.div(c, boxes), lax.rem(c, boxes)
-
-        @pl.when(h == 0)
-        def _():
-            for where in range(nz):
-                prepare_interp(where, k)
-
-        for j in range(1, nz):
-            from_z(c, j).wait_recv()
-        for where in range(nz):
-            samples = mul3(zgot[c, where], ip[where, k], 2 * q)
+                from_z(c, j).wait_recv()
+        jobs = [(c, where) for c in group for where in range(nz)]
+        samples = [mul3(zgot[c, where], ip[where, box(c)[1]], 2 * q) for c, where in jobs]
+        for (c, where), sample in zip(jobs, samples):
+            h, k = box(c)
             for part in range(2):
                 flat = stage.at[h, part].reshape(rows * boxes, q)
-                flat[pl.ds(where * boxes + k, zrows, stride=nz * boxes), :] = samples[
+                flat[pl.ds(where * boxes + k, zrows, stride=nz * boxes), :] = sample[
                     :, part * q:(part + 1) * q]
+
+        h, k = box(group[-1])
 
         @pl.when(k == boxes - 1)
         def _():
@@ -244,8 +259,8 @@
             lax.fori_loop(1, plane, send, 0)
             keep(h).start()
 
-    ahead, apart = boxes, 3
-    lag = [0] + [ahead + apart * (level - 1) for level in range(1, levels + 1)]
+    steps = chunks // GROUP
+    lag = [0, 3, 5] + [7 + level for level in range(levels - 3)] + [levels + 5]
 
     def tick(t, _):
         for j in range(nz):
@@ -254,18 +269,18 @@
                 gather_step(j)
 
         for level in range(levels + 1):
-            c = t - lag[level]
-
-            @pl.when((t >= lag[level]) & (t < lag[level] + chunks))
+            step = t - lag[level]
+
+            @pl.when((t >= lag[level]) & (t < lag[level] + steps))
             def _():
                 if level < levels:
-                    work(level, c)
+                    work(level, step)
                 else:
-                    project(c)
-
-        return 0
-
-    lax.fori_loop(0, chunks + lag[-1], tick, 0)
+                    project(step)
+
+        return 0
+
+    lax.fori_loop(0, steps + lag[-1], tick, 0)
 
     def finish(c, _):
         for level in range(max(levels + 1 - SLOTS, 0), levels):

time: 219 us -> 216 us (0.986)
  no operation moved by 1% of the time
where the time goes in v2:
time: 216 us; the launch traced here: 215 us
  Pallas kernels  211 us (98%)
  local copies, waits for them, and re-layouts  4.65 us (2%)
    pallas_call x1, Pallas kernels, on_device(): pl.pallas_call(functools.partial(kernel, ngx, ngy, parts), out_shape=jax....  211 us
    unnamed x1, local copies, waits for them, and re-layouts  4.65 us

profile of v2, /device:TPU:1, one launch (start us, length us, event | category | flops | bytes accessed | tf_op | source)
XLA Modules:
  0.0 215.4 jit_solution(13165744961581016904)
XLA Ops:
  0.0 210.8 %shard_map.37 = f32[2,16,4,4,2,8,128]{6,5,4,3,2,1,0:T(8,128)} custom-call(f32[2,8,64,512]{3,2,1,0:T(8,128)} %source.1, f32[5,2,8,64,128]{4,3,2,1,0:T(8,128)} %weights.1, f32[2,8,64,128]{3,2,1,0:T(8,128)} %interp.1), custom_call_target="tpu_custom_call" | custom-call | tf_op jit(solution)/shard_map/pallas_call | solution.py:327
  210.8 4.7 %copy.5 = f32[2,16,256,128]{3,2,1,0:T(8,128)} copy(f32[2,16,256,128]{3,2,1,0:T(8,128)} %bitcast.1) | data formatting | bytes 8388608

commit v3 on v2

--- a/solution.py
+++ b/solution.py
@@ -184,20 +184,15 @@
                         held[0, h * boxes + k, to:to + ngx, :] = turned[
                             pl.ds(start, ngx, stride=ngy * each), :]
 
-    turn(0)
-    igot[z] = interp[...]
-    pl.semaphore_wait(barrier, nz - 1 + plane - 1)
-
-    def begin(k, _):
-        @pl.when(k > 0)
-        def _():
-            turn(k)
+    def begin(step):
+        @pl.when(step > 0)
+        def _():
+            for g in range(GROUP):
+                turn(step * GROUP + g)
 
         for h in range(parts):
-            exchange(0, h * boxes + k).start()
-        return 0
-
-    lax.fori_loop(0, boxes, begin, 0)
+            for g in range(GROUP):
+                exchange(0, h * boxes + step * GROUP + g).start()
 
     def box(c):
         return lax.div(c, boxes), lax.rem(c, boxes)
@@ -260,24 +255,39 @@
             keep(h).start()
 
     steps = chunks // GROUP
-    lag = [0, 3, 5] + [7 + level for level in range(levels - 3)] + [levels + 5]
+    lag = [1, 3, 5] + [7 + level for level in range(levels - 3)] + [levels + 5]
+    gather_from, catch_up = 5, 16
+    for g in range(GROUP):
+        turn(g)
+    igot[z] = interp[...]
+    pl.semaphore_wait(barrier, nz - 1 + plane - 1)
+
+    def projected(t):
+        done = jnp.minimum(2 * (t - catch_up + 1), t - lag[-1] + 1)
+        return jnp.clip(done, 0, steps)
 
     def tick(t, _):
         for j in range(nz):
-            @pl.when(t == j * lag[-1] // max(nz - 1, 1))
+            @pl.when(t == gather_from + j * (catch_up - gather_from) // max(nz - 1, 1))
             def _():
                 gather_step(j)
 
-        for level in range(levels + 1):
+        @pl.when(t < boxes // GROUP)
+        def _():
+            begin(t)
+
+        for level in range(levels):
             step = t - lag[level]
 
             @pl.when((t >= lag[level]) & (t < lag[level] + steps))
             def _():
-                if level < levels:
-                    work(level, step)
-                else:
-                    project(step)
-
+                work(level, step)
+
+        def late(step, _):
+            project(step)
+            return 0
+
+        lax.fori_loop(projected(t - 1), projected(t), late, 0)
         return 0
 
     lax.fori_loop(0, steps + lag[-1], tick, 0)

time: 216 us -> 221 us (1.023)
  Pallas kernels: 211 us -> 216 us
    pallas_call x1, Pallas kernels: 211 us -> 216 us  [on_device(): pl.pallas_call(functools.partial(kernel, ngx, ngy, parts), out_shape=jax....]
where the time goes in v3:
time: 221 us
  Pallas kernels  216 us (98%)
  local copies, waits for them, and re-layouts  4.65 us (2%)
    pallas_call x1, Pallas kernels, on_device(): pl.pallas_call(functools.partial(kernel, ngx, ngy, parts), out_shape=jax....  216 us
    unnamed x1, local copies, waits for them, and re-layouts  4.65 us

profile of v3, /device:TPU:1, one launch (start us, length us, event | category | flops | bytes accessed | tf_op | source)
XLA Modules:
  0.0 221.0 jit_solution(6730571673773940031)
XLA Ops:
  0.0 216.3 %shard_map.37 = f32[2,16,4,4,2,8,128]{6,5,4,3,2,1,0:T(8,128)} custom-call(f32[2,8,64,512]{3,2,1,0:T(8,128)} %source.1, f32[5,2,8,64,128]{4,3,2,1,0:T(8,128)} %weights.1, f32[2,8,64,128]{3,2,1,0:T(8,128)} %interp.1), custom_call_target="tpu_custom_call" | custom-call | tf_op jit(solution)/shard_map/pallas_call | solution.py:337
  216.3 4.7 %copy.5 = f32[2,16,256,128]{3,2,1,0:T(8,128)} copy(f32[2,16,256,128]{3,2,1,0:T(8,128)} %bitcast.1) | data formatting | bytes 8388608

commit v4 on v3

--- a/solution.py
+++ b/solution.py
@@ -12,7 +12,7 @@
 F32 = jnp.float32
 CORES = 2
 SLOTS = 3
-GROUP = 2
+GROUP = 1
 
 
 def split(x):
@@ -256,7 +256,7 @@
 
     steps = chunks // GROUP
     lag = [1, 3, 5] + [7 + level for level in range(levels - 3)] + [levels + 5]
-    gather_from, catch_up = 5, 16
+    gather_from, catch_up = 1, 13
     for g in range(GROUP):
         turn(g)
     igot[z] = interp[...]
@@ -329,7 +329,7 @@
         levels = weights.shape[0]
         q = interp.shape[3]
         each = frames // n
-        parts = 4 if each % 4 == 0 else 1
+        parts = 2 if each % 2 == 0 else 1
         rows = frames // parts
         chunks = parts * boxes
         vmem = pl.BlockSpec(memory_space=pltpu.VMEM)

time: 221 us -> 216 us (0.977)
  Pallas kernels: 216 us -> 211 us
    pallas_call x1, Pallas kernels: 216 us -> 211 us  [on_device(): pl.pallas_call(functools.partial(kernel, ngx, ngy, parts), out_shape=jax....]
where the time goes in v4:
time: 216 us
  Pallas kernels  211 us (98%)
  local copies, waits for them, and re-layouts  4.65 us (2%)
    pallas_call x1, Pallas kernels, on_device(): pl.pallas_call(functools.partial(kernel, ngx, ngy, parts), out_shape=jax....  211 us
    unnamed x1, local copies, waits for them, and re-layouts  4.65 us

profile of v4, /device:TPU:1, one launch (start us, length us, event | category | flops | bytes accessed | tf_op | source)
XLA Modules:
  0.0 215.8 jit_solution(1663674889542084613)
XLA Ops:
  0.0 211.1 %shard_map.37 = f32[2,16,4,4,2,8,128]{6,5,4,3,2,1,0:T(8,128)} custom-call(f32[2,8,64,512]{3,2,1,0:T(8,128)} %source.1, f32[5,2,8,64,128]{4,3,2,1,0:T(8,128)} %weights.1, f32[2,8,64,128]{3,2,1,0:T(8,128)} %interp.1), custom_call_target="tpu_custom_call" | custom-call | tf_op jit(solution)/shard_map/pallas_call | solution.py:337
  211.1 4.7 %copy.5 = f32[2,16,256,128]{3,2,1,0:T(8,128)} copy(f32[2,16,256,128]{3,2,1,0:T(8,128)} %bitcast.1) | data formatting | bytes 8388608

commit v5 on v4

--- a/solution.py
+++ b/solution.py
@@ -255,7 +255,8 @@
             keep(h).start()
 
     steps = chunks // GROUP
-    lag = [1, 3, 5] + [7 + level for level in range(levels - 3)] + [levels + 5]
+    lag = [1 + 2 * level for level in range(levels + 1)]
+    shift = 3 * core + 2 * lax.rem(z, 2)
     gather_from, catch_up = 1, 13
     for g in range(GROUP):
         turn(g)
@@ -276,18 +277,26 @@
         def _():
             begin(t)
 
-        for level in range(levels):
-            step = t - lag[level]
-
-            @pl.when((t >= lag[level]) & (t < lag[level] + steps))
-            def _():
-                work(level, step)
-
         def late(step, _):
             project(step)
             return 0
 
-        lax.fori_loop(projected(t - 1), projected(t), late, 0)
+        def visit(i, _):
+            turn_of = lax.rem(i + shift, levels + 1)
+            for level in range(levels):
+                step = t - lag[level]
+
+                @pl.when((turn_of == level) & (t >= lag[level]) & (t < lag[level] + steps))
+                def _():
+                    work(level, step)
+
+            @pl.when(turn_of == levels)
+            def _():
+                lax.fori_loop(projected(t - 1), projected(t), late, 0)
+
+            return 0
+
+        lax.fori_loop(0, levels + 1, visit, 0)
         return 0
 
     lax.fori_loop(0, steps + lag[-1], tick, 0)

time: 216 us -> 223 us (1.032)
  Pallas kernels: 211 us -> 218 us
    pallas_call x1, Pallas kernels: 211 us -> 218 us  [on_device(): pl.pallas_call(functools.partial(kernel, ngx, ngy, parts), out_shape=jax....]
where the time goes in v5:
time: 223 us; the launch traced here: 222 us
  Pallas kernels  218 us (98%)
  local copies, waits for them, and re-layouts  4.65 us (2%)
    pallas_call x1, Pallas kernels, on_device(): pl.pallas_call(functools.partial(kernel, ngx, ngy, parts), out_shape=jax....  218 us
    unnamed x1, local copies, waits for them, and re-layouts  4.65 us

profile of v5, /device:TPU:1, one launch (start us, length us, event | category | flops | bytes accessed | tf_op | source)
XLA Modules:
  0.0 222.5 jit_solution(12082453837996573267)
XLA Ops:
  0.0 217.8 %shard_map.37 = f32[2,16,4,4,2,8,128]{6,5,4,3,2,1,0:T(8,128)} custom-call(f32[2,8,64,512]{3,2,1,0:T(8,128)} %source.1, f32[5,2,8,64,128]{4,3,2,1,0:T(8,128)} %weights.1, f32[2,8,64,128]{3,2,1,0:T(8,128)} %interp.1), custom_call_target="tpu_custom_call" | custom-call | tf_op jit(solution)/shard_map/pallas_call | solution.py:346
  217.8 4.7 %copy.5 = f32[2,16,256,128]{3,2,1,0:T(8,128)} copy(f32[2,16,256,128]{3,2,1,0:T(8,128)} %bitcast.1) | data formatting | bytes 8388608

commit v6 on v3

--- a/solution.py
+++ b/solution.py
@@ -97,26 +97,26 @@
         wp[level, k] = jnp.concatenate([hi, lo], axis=1)
 
     def prepare_interp(where, k):
-        real, imag = igot[where, 0, k], igot[where, 1, k]
+        real, imag = igot[where, k, 0], igot[where, k, 1]
         top = jnp.concatenate([real, imag], axis=1)
         low = jnp.concatenate([-imag, real], axis=1)
         hi, lo = split(jnp.concatenate([top, low], axis=0))
         ip[where, k] = jnp.concatenate([hi, lo], axis=1)
 
-    def pass_on(way, j):
+    def pass_on(way, j, k):
         block = z - j if way == 0 else z + j
         there = z + 1 if way == 0 else z - 1
         return pltpu.make_async_remote_copy(
-            src_ref=igot.at[block], dst_ref=igot.at[block],
-            send_sem=isend_sem.at[way, j], recv_sem=irecv_sem.at[way, j + 1],
+            src_ref=igot.at[block, k], dst_ref=igot.at[block, k],
+            send_sem=isend_sem.at[way, j, k], recv_sem=irecv_sem.at[way, j + 1, k],
             device_id=at_z(there), device_id_type=MESH)
 
-    def taken(way, j):
+    def taken(way, j, k):
         block = z - j if way == 0 else z + j
         there = z - 1 if way == 0 else z + 1
         return pltpu.make_async_remote_copy(
-            src_ref=igot.at[block], dst_ref=igot.at[block],
-            send_sem=isend_sem.at[way, j - 1], recv_sem=irecv_sem.at[way, j],
+            src_ref=igot.at[block, k], dst_ref=igot.at[block, k],
+            send_sem=isend_sem.at[way, j - 1, k], recv_sem=irecv_sem.at[way, j, k],
             device_id=at_z(there), device_id_type=MESH)
 
     def sends(way, j):
@@ -125,16 +125,18 @@
     def takes(way, j):
         return (z >= j) if way == 0 else (z + j < nz)
 
-    def gather_step(j):
+    def gather_step(j, step):
         for way in range(2):
-            if j > 0:
-                @pl.when(takes(way, j))
-                def _():
-                    taken(way, j).wait_recv()
-            if j < nz - 1:
-                @pl.when(sends(way, j))
-                def _():
-                    pass_on(way, j).start()
+            for g in range(GROUP):
+                k = step * GROUP + g
+                if j > 0:
+                    @pl.when(takes(way, j))
+                    def _():
+                        taken(way, j, k).wait_recv()
+                if j < nz - 1:
+                    @pl.when(sends(way, j))
+                    def _():
+                        pass_on(way, j, k).start()
 
     def over_z(c, j):
         there = lax.rem(z + j, nz)
@@ -256,38 +258,37 @@
 
     steps = chunks // GROUP
     lag = [1, 3, 5] + [7 + level for level in range(levels - 3)] + [levels + 5]
-    gather_from, catch_up = 5, 16
+    gap = (lag[-1] - 1) // max(nz - 1, 1)
     for g in range(GROUP):
         turn(g)
-    igot[z] = interp[...]
+    for k in range(boxes):
+        for part in range(2):
+            igot[z, k, part] = interp[part, k]
     pl.semaphore_wait(barrier, nz - 1 + plane - 1)
 
-    def projected(t):
-        done = jnp.minimum(2 * (t - catch_up + 1), t - lag[-1] + 1)
-        return jnp.clip(done, 0, steps)
-
     def tick(t, _):
-        for j in range(nz):
-            @pl.when(t == gather_from + j * (catch_up - gather_from) // max(nz - 1, 1))
-            def _():
-                gather_step(j)
-
         @pl.when(t < boxes // GROUP)
         def _():
             begin(t)
 
-        for level in range(levels):
+        for level in range(levels + 1):
             step = t - lag[level]
 
             @pl.when((t >= lag[level]) & (t < lag[level] + steps))
             def _():
-                work(level, step)
-
-        def late(step, _):
-            project(step)
-            return 0
-
-        lax.fori_loop(projected(t - 1), projected(t), late, 0)
+                if level < levels:
+                    work(level, step)
+                else:
+                    project(step)
+
+            if level == min(2, levels):
+                for j in range(nz):
+                    start = 1 + j * gap
+
+                    @pl.when((t >= start) & (t < start + boxes // GROUP))
+                    def _():
+                        gather_step(j, t - start)
+
         return 0
 
     lax.fori_loop(0, steps + lag[-1], tick, 0)
@@ -304,7 +305,8 @@
         for j in range(nz - 1):
             @pl.when(sends(way, j))
             def _():
-                pass_on(way, j).wait_send()
+                for k in range(boxes):
+                    pass_on(way, j, k).wait_send()
 
     def end(h, _):
         def one(i, _):
@@ -345,15 +347,15 @@
                 pltpu.VMEM((SLOTS, chunks, rows, 2 * rank), F32),
                 pltpu.VMEM((levels, chunks, rows, 2 * rank), F32),
                 pltpu.VMEM((chunks, nz, rows // nz, 2 * rank), F32),
-                pltpu.VMEM((nz,) + interp.shape, F32),
+                pltpu.VMEM((nz, boxes, 2, rank, q), F32),
                 pltpu.VMEM((parts, 2, each // parts, CORES, ngx, nz, boxes, q), F32),
                 pltpu.VMEM((frames, 2 * rank), F32),
                 dma((levels, chunks)),
                 dma((levels, chunks)),
                 dma((chunks, nz)),
                 dma((chunks, nz)),
-                dma((2, nz)),
-                dma((2, nz)),
+                dma((2, nz, boxes)),
+                dma((2, nz, boxes)),
                 dma((parts, CORES * ngx)),
                 dma((parts, CORES * ngx)),
                 dma((parts,)),

time: 221 us -> 214 us (0.968)
  Pallas kernels: 216 us -> 209 us
    pallas_call x1, Pallas kernels: 216 us -> 209 us  [on_device(): pl.pallas_call(functools.partial(kernel, ngx, ngy, parts), out_shape=jax....]
where the time goes in v6:
time: 214 us; the launch traced here: 213 us
  Pallas kernels  209 us (98%)
  local copies, waits for them, and re-layouts  4.65 us (2%)
    pallas_call x1, Pallas kernels, on_device(): pl.pallas_call(functools.partial(kernel, ngx, ngy, parts), out_shape=jax....  209 us
    unnamed x1, local copies, waits for them, and re-layouts  4.65 us

profile of v6, /device:TPU:1, one launch (start us, length us, event | category | flops | bytes accessed | tf_op | source)
XLA Modules:
  0.0 213.5 jit_solution(5939152713295537913)
XLA Ops:
  0.0 208.8 %shard_map.37 = f32[2,16,4,4,2,8,128]{6,5,4,3,2,1,0:T(8,128)} custom-call(f32[2,8,64,512]{3,2,1,0:T(8,128)} %source.1, f32[5,2,8,64,128]{4,3,2,1,0:T(8,128)} %weights.1, f32[2,8,64,128]{3,2,1,0:T(8,128)} %interp.1), custom_call_target="tpu_custom_call" | custom-call | tf_op jit(solution)/shard_map/pallas_call | solution.py:339
  208.8 4.7 %copy.5 = f32[2,16,256,128]{3,2,1,0:T(8,128)} copy(f32[2,16,256,128]{3,2,1,0:T(8,128)} %bitcast.1) | data formatting | bytes 8388608

commit v7 on v6

--- a/solution.py
+++ b/solution.py
@@ -257,7 +257,7 @@
             keep(h).start()
 
     steps = chunks // GROUP
-    lag = [1, 3, 5] + [7 + level for level in range(levels - 3)] + [levels + 5]
+    lag = [1, 4, 8] + [11 + 2 * level for level in range(levels - 3)] + [2 * levels + 6]
     gap = (lag[-1] - 1) // max(nz - 1, 1)
     for g in range(GROUP):
         turn(g)

time: 214 us -> 227 us (1.061)
  Pallas kernels: 209 us -> 222 us
    pallas_call x1, Pallas kernels: 209 us -> 222 us  [on_device(): pl.pallas_call(functools.partial(kernel, ngx, ngy, parts), out_shape=jax....]
where the time goes in v7:
time: 227 us
  Pallas kernels  222 us (98%)
  local copies, waits for them, and re-layouts  4.65 us (2%)
    pallas_call x1, Pallas kernels, on_device(): pl.pallas_call(functools.partial(kernel, ngx, ngy, parts), out_shape=jax....  222 us
    unnamed x1, local copies, waits for them, and re-layouts  4.65 us

profile of v7, /device:TPU:1, one launch (start us, length us, event | category | flops | bytes accessed | tf_op | source)
XLA Modules:
  0.0 227.1 jit_solution(9990367372540957119)
XLA Ops:
  0.0 222.4 %shard_map.37 = f32[2,16,4,4,2,8,128]{6,5,4,3,2,1,0:T(8,128)} custom-call(f32[2,8,64,512]{3,2,1,0:T(8,128)} %source.1, f32[5,2,8,64,128]{4,3,2,1,0:T(8,128)} %weights.1, f32[2,8,64,128]{3,2,1,0:T(8,128)} %interp.1), custom_call_target="tpu_custom_call" | custom-call | tf_op jit(solution)/shard_map/pallas_call | solution.py:339
  222.4 4.7 %copy.5 = f32[2,16,256,128]{3,2,1,0:T(8,128)} copy(f32[2,16,256,128]{3,2,1,0:T(8,128)} %bitcast.1) | data formatting | bytes 8388608

commit v8 on v7

--- a/solution.py
+++ b/solution.py
@@ -257,7 +257,7 @@
             keep(h).start()
 
     steps = chunks // GROUP
-    lag = [1, 4, 8] + [11 + 2 * level for level in range(levels - 3)] + [2 * levels + 6]
+    lag = [1, 2] + [4 + level for level in range(levels - 1)]
     gap = (lag[-1] - 1) // max(nz - 1, 1)
     for g in range(GROUP):
         turn(g)

time: 227 us -> 220 us (0.969)
  Pallas kernels: 222 us -> 215 us
    pallas_call x1, Pallas kernels: 222 us -> 215 us  [on_device(): pl.pallas_call(functools.partial(kernel, ngx, ngy, parts), out_shape=jax....]
where the time goes in v8:
time: 220 us; the launch traced here: 219 us
  Pallas kernels  215 us (98%)
  local copies, waits for them, and re-layouts  4.65 us (2%)
    pallas_call x1, Pallas kernels, on_device(): pl.pallas_call(functools.partial(kernel, ngx, ngy, parts), out_shape=jax....  215 us
    unnamed x1, local copies, waits for them, and re-layouts  4.65 us

profile of v8, /device:TPU:1, one launch (start us, length us, event | category | flops | bytes accessed | tf_op | source)
XLA Modules:
  0.0 219.4 jit_solution(5796637252763286344)
XLA Ops:
  0.0 214.7 %shard_map.37 = f32[2,16,4,4,2,8,128]{6,5,4,3,2,1,0:T(8,128)} custom-call(f32[2,8,64,512]{3,2,1,0:T(8,128)} %source.1, f32[5,2,8,64,128]{4,3,2,1,0:T(8,128)} %weights.1, f32[2,8,64,128]{3,2,1,0:T(8,128)} %interp.1), custom_call_target="tpu_custom_call" | custom-call | tf_op jit(solution)/shard_map/pallas_call | solution.py:339
  214.7 4.7 %copy.5 = f32[2,16,256,128]{3,2,1,0:T(8,128)} copy(f32[2,16,256,128]{3,2,1,0:T(8,128)} %bitcast.1) | data formatting | bytes 8388608

commit v9 on v6

--- a/solution.py
+++ b/solution.py
@@ -12,7 +12,7 @@
 F32 = jnp.float32
 CORES = 2
 SLOTS = 3
-GROUP = 2
+GROUP = 1
 
 
 def split(x):
@@ -331,7 +331,7 @@
         levels = weights.shape[0]
         q = interp.shape[3]
         each = frames // n
-        parts = 4 if each % 4 == 0 else 1
+        parts = 2 if each % 2 == 0 else 1
         rows = frames // parts
         chunks = parts * boxes
         vmem = pl.BlockSpec(memory_space=pltpu.VMEM)

time: 214 us -> 225 us (1.051)
  Pallas kernels: 209 us -> 221 us
    pallas_call x1, Pallas kernels: 209 us -> 221 us  [on_device(): pl.pallas_call(functools.partial(kernel, ngx, ngy, parts), out_shape=jax....]
where the time goes in v9:
time: 225 us
  Pallas kernels  221 us (98%)
  local copies, waits for them, and re-layouts  4.65 us (2%)
    pallas_call x1, Pallas kernels, on_device(): pl.pallas_call(functools.partial(kernel, ngx, ngy, parts), out_shape=jax....  221 us
    unnamed x1, local copies, waits for them, and re-layouts  4.65 us

profile of v9, /device:TPU:1, one launch (start us, length us, event | category | flops | bytes accessed | tf_op | source)
XLA Modules:
  0.0 225.2 jit_solution(10971187780466476166)
XLA Ops:
  0.0 220.6 %shard_map.37 = f32[2,16,4,4,2,8,128]{6,5,4,3,2,1,0:T(8,128)} custom-call(f32[2,8,64,512]{3,2,1,0:T(8,128)} %source.1, f32[5,2,8,64,128]{4,3,2,1,0:T(8,128)} %weights.1, f32[2,8,64,128]{3,2,1,0:T(8,128)} %interp.1), custom_call_target="tpu_custom_call" | custom-call | tf_op jit(solution)/shard_map/pallas_call | solution.py:339
  220.6 4.7 %copy.5 = f32[2,16,256,128]{3,2,1,0:T(8,128)} copy(f32[2,16,256,128]{3,2,1,0:T(8,128)} %bitcast.1) | data formatting | bytes 8388608
